TPU v7x, 32 devices: a whole 2x2x4 slice. The times are simulated.
32 devices in a mesh: section: 2 (over z_hi), dp: 8 (over y, x, core), tensor: 2 (over z_lo).
Axes of the slice: x: 2, y: 2, z: 4 (z_hi: 2, z_lo: 2; z = z_hi * 2 + z_lo), core: 2. Of those that a mesh axis runs over, the one named last changes fastest.
Arguments:
- hidden_in: bfloat16 [2, 1024, 8192], P('section', ('dp', 'tensor')), may hold values from -600 to 600
- norm_gain: bfloat16 [2, 8192], P('section'), may hold values from 0.5 to 1.5
- value_weight: bfloat16 [2, 8192, 512], P('section', 'dp', 'tensor'), may hold values from -0.0625 to 0.0625
- query_vectors: bfloat16 [2, 1024, 4096], P('section', 'dp', 'tensor'), may hold values from -9 to 9
- key_vectors: bfloat16 [2, 1024, 512], P('section', 'dp', 'tensor'), may hold values from -9 to 9
- grad_attn: bfloat16 [2, 1024, 4096], P('section', 'dp', 'tensor'), may hold values from -250 to 250
- positions: int32 [2, 1024], P('section', 'dp'), may hold values from 0 to 65535, as said below
Outputs:
- value_weight_grad: float32 [2, 8192, 512], P('section', 'dp', 'tensor')
- norm_gain_grad: float32 [2, 8192], P('section')
- to_previous: bfloat16 [2, 1024, 8192], P('section', ('dp', 'tensor'))
Inputs may be any that keep to these rules, and one draw needn't show every extreme that they name: Within each micro-batch of 128 rows, positions rise by one from row to row except at one row between row 32 and row 95, where a new document starts at position 0.
All inputs are finite; a program needn't handle non-finite values.
Results may differ from a plain program's by a relative error of at most 0.014.
Values may be sent and summed in bfloat16 or wider, within the bound.
A program may use at most 64 MiB of HBM per device.

v0:
```python
import math

import jax
import jax.numpy as jnp
from jax import lax
from jax.sharding import PartitionSpec as P

HD = 128
QPK = 8


def shifted(value, axis, steps):
    count = lax.axis_size(axis)
    first, last = (max(0, -steps), min(count, count - steps))
    return lax.ppermute(value, axis, [(source, source + steps) for source in range(first, last)])


def attend(query_rows, key_rows, grad_rows, position_rows):
    length = query_rows.shape[0]
    groups = key_rows.shape[1] // HD
    query_heads = query_rows.reshape(length, groups, QPK, HD)
    key_heads = key_rows.reshape(length, groups, HD)
    grad_heads = grad_rows.reshape(length, groups, QPK, HD)
    scores = jnp.einsum(
        "igpd,jgd->gpij", query_heads, key_heads, preferred_element_type=jnp.float32
    ) / math.sqrt(HD)
    places = jnp.arange(length, dtype=jnp.int32)
    visible = (places[:, None] >= places[None, :]) & (
        position_rows[:, None] - position_rows[None, :] == places[:, None] - places[None, :]
    )
    masked = jnp.where(visible, scores, jnp.float32(-1e30))
    largest = jnp.max(masked, axis=-1, keepdims=True)
    powers = jnp.where(visible, jnp.exp(masked - largest), jnp.float32(0.0))
    probabilities = powers / jnp.sum(powers, axis=-1, keepdims=True)
    weights = probabilities.astype(jnp.bfloat16)
    value_grad = jnp.einsum(
        "gpij,igpd->jgd", weights, grad_heads, preferred_element_type=jnp.float32
    )
    return value_grad.reshape(length, groups * HD).astype(jnp.bfloat16)


def shards(hidden_in, norm_gain, value_weight, query_vectors, key_vectors, grad_attn, positions):
    rows_float = hidden_in[0].astype(jnp.float32)
    root_mean = jnp.sqrt(jnp.mean(rows_float * rows_float, axis=1, keepdims=True) + 1e-05)
    normed = rows_float / root_mean
    gain_float = norm_gain[0].astype(jnp.float32)
    own_input = (normed * gain_float).astype(jnp.bfloat16)
    layer_input = lax.all_gather(own_input, "tensor", axis=0, tiled=True)
    value_grad = attend(query_vectors[0], key_vectors[0], grad_attn[0], positions[0])
    local_weight = value_weight[0]
    weight_grad = lax.psum_scatter(
        jnp.einsum("tc,tk->ck", layer_input, value_grad, preferred_element_type=jnp.float32).astype(
            jnp.bfloat16
        ),
        "dp",
        scatter_dimension=0,
        tiled=True,
    ).astype(jnp.float32)
    input_part = jnp.einsum(
        "tk,ck->tc",
        value_grad,
        lax.all_gather(local_weight, "dp", axis=0, tiled=True),
        preferred_element_type=jnp.float32,
    ).astype(jnp.bfloat16)
    own_rows = hidden_in.shape[1]
    stacked = input_part.reshape(lax.axis_size("tensor"), own_rows, input_part.shape[1])
    arrived = lax.all_to_all(stacked, "tensor", split_axis=0, concat_axis=0, tiled=True)
    own_grad = jnp.sum(arrived.astype(jnp.float32), axis=0)
    grad_normed = own_grad * gain_float
    inner_mean = jnp.mean(grad_normed * normed, axis=1, keepdims=True)
    grad_hidden = ((grad_normed - normed * inner_mean) / root_mean).astype(jnp.bfloat16)
    gain_grad = lax.psum(jnp.sum(own_grad * normed, axis=0), ("dp", "tensor"))
    to_previous = shifted(grad_hidden, "section", -1)
    return (weight_grad[None], gain_grad[None], to_previous[None])


def solution(mesh):
    placed = (
        P("section", ("dp", "tensor"), None),
        P("section", None),
        P("section", "dp", "tensor"),
        P("section", "dp", "tensor"),
        P("section", "dp", "tensor"),
        P("section", "dp", "tensor"),
        P("section", "dp"),
    )
    return jax.shard_map(
        shards,
        mesh=mesh,
        in_specs=placed,
        out_specs=(
            P("section", "dp", "tensor"),
            P("section", None),
            P("section", ("dp", "tensor"), None),
        ),
        check_vma=False,
    )
```

profile of v0, /device:TPU:1, one launch (start us, length us, event | category | flops | bytes accessed | tf_op | source)
XLA Modules:
  0.0 202.5 jit_solution(17997017190973721375)
XLA Ops:
  7.2 0.0 copy-start.2
  7.2 0.0 all-gather.6.cloned.1.call-start
  7.2 0.7 all-gather.6.cloned.1.call-update
  7.9 0.9 reshape_squeeze.9
  8.8 1.1 copy.20
  9.9 1.3 copy.19
  11.2 0.0 copy-done.2
  11.3 0.1 fusion.11
  11.3 0.5 fusion.23
  11.9 0.3 fusion.8
  12.2 37.0 %all-gather.6.cloned.1.call-done = bf16[1,8192,256]{2,1,0:T(8,128)(2,1)} async-done(((bf16[1,1024,256]{2,1,0:T(8,128)(2,1)}), bf16[1,8192,256]{2,1,0:T(8,128)(2,1)}) %all-gather.6.cloned.1.call-update) | async-done | bytes 4194320 | tf_op jit(solution)/shard_map/all_gather | solution.py:62
  49.2 5.0 %convolution_convert_fusion.1 = bf16[128,8192]{1,0:T(8,128)(2,1)} fusion(bf16[128,256]{0,1:T(8,128)(2,1)S(1)} %bitcast.57, bf16[1,8192,256]{2,1,0:T(8,128)(2,1)} %all-gather.6.cloned.1.call-done), kind=kOutput, calls=%fused_computation.2 | convolution fusion | flops 537919488 | bytes 6356992 | tf_op jit(solution)/shard_map/tk,ck->tc/dot_general | solution.py:59
  54.2 0.0 copy-start.1
  54.2 0.0 copy-start
  54.2 3.9 %all-to-all-start = ((bf16[2,64,8192]{2,1,0:T(8,128)(2,1)}), bf16[2,64,8192]{2,1,0:T(8,128)(2,1)S(1)}, u32[]{:S(2)}, u32[]{:S(2)}) async-start(bf16[2,64,8192]{2,1,0:T(8,128)(2,1)} %bitcast.14), calls=%async_computation.1 | async-start | bytes 4194304 | tf_op jit(solution)/shard_map/all_to_all | solution.py:67
  58.1 0.0 all-gather.4.cloned.1.call-start
  58.1 0.0 copy-done.1
  58.2 0.0 copy-done
  58.2 0.3 fusion.2
  58.5 24.3 %all-to-all-done = bf16[2,64,8192]{2,1,0:T(8,128)(2,1)S(1)} async-done(((bf16[2,64,8192]{2,1,0:T(8,128)(2,1)}), bf16[2,64,8192]{2,1,0:T(8,128)(2,1)S(1)}, u32[]{:S(2)}, u32[]{:S(2)}) %all-to-all-start) | async-done | bytes 2097184 | tf_op jit(solution)/shard_map/all_to_all | solution.py:67
  82.8 0.3 convert_reduce_fusion
  83.1 0.9 multiply_reduce_fusion
  84.0 1.6 divide_convert_fusion
  85.6 0.0 all-gather.4.cloned.1.call-update
  85.7 0.0 reduce-scatter.2.cloned.1.call-start
  85.7 32.7 %all-gather.4.cloned.1.call-done = bf16[128,8192]{1,0:T(8,128)(2,1)} async-done(((bf16[64,8192]{1,0:T(8,128)(2,1)}), bf16[128,8192]{1,0:T(8,128)(2,1)}) %all-gather.4.cloned.1.call-update) | async-done | bytes 2097168 | tf_op jit(solution)/shard_map/all_gather | solution.py:48
  118.4 4.8 %convolution_convert_fusion = bf16[8192,256]{1,0:T(8,128)(2,1)} fusion(bf16[128,8192]{1,0:T(8,128)(2,1)} %all-gather.4.cloned.1.call-done, bf16[128,256]{0,1:T(8,128)(2,1)S(1)} %bitcast.58), kind=kOutput, calls=%fused_computation.1 | convolution fusion | flops 538968064 | bytes 6356992 | tf_op jit(solution)/shard_map/tc,tk->ck/dot_general | solution.py:52
  123.2 0.0 reduce-scatter.2.cloned.1.call-update
  123.2 1.3 collective-permute-start
  124.5 68.4 %psum.7 = f32[1,8192]{1,0:T(1,128)} all-reduce(f32[1,8192]{1,0:T(1,128)S(1)} %bitcast.59), channel_id=1, replica_groups=mesh['section'=2,'dp'=8,'tensor'=2] {'dp','tensor'}, use_global_device_ids=true, to_apply=%region_6.7 | all-reduce | flops 8192 | bytes 65536 | tf_op jit(solution)/shard_map/psum | solution.py:72
  192.9 0.0 collective-permute-done
  193.0 0.0 reduce-scatter.2.cloned.1.call-done
  193.0 2.1 %bitcast_convert_fusion = f32[1,1024,256]{2,1,0:T(8,128)} fusion(bf16[1024,256]{1,0:T(8,128)(2,1)} %reduce-scatter.2.cloned.1.call-done), kind=kLoop, calls=%fused_computation.21 | loop fusion | flops 262144 | bytes 1572864 | tf_op jit(solution)/shard_map/broadcast_in_dim | solution.py:74
  195.0 1.0 copy.38
  (3 shorter events, 0.1 us)
Async XLA Ops:
  7.2 4.1 %copy-start.2 = (s32[1,128]{1,0:T(1,128)S(1)}, s32[1,128]{1,0:T(1,128)}, u32[]{:S(2)}) copy-start(s32[1,128]{1,0:T(1,128)} %param.13) | copy-start | bytes 1540
  7.2 42.0 %all-gather.6.cloned.1.call-start = ((), (), s32[]{:S(2)}) async-start(), calls=%async_computation.4 | async-start | bytes 4718592 | tf_op jit(solution)/shard_map/all_gather | solution.py:62
  54.2 4.0 %copy-start.1 = (bf16[1,8192]{1,0:T(2,128)(2,1)S(1)}, bf16[1,8192]{1,0:T(2,128)(2,1)}, u32[]{:S(2)}) copy-start(bf16[1,8192]{1,0:T(2,128)(2,1)} %param.8) | copy-start | bytes 49156
  54.2 4.0 %copy-start = (bf16[1,64,8192]{2,1,0:T(8,128)(2,1)S(1)}, bf16[1,64,8192]{2,1,0:T(8,128)(2,1)}, u32[]{:S(2)}) copy-start(bf16[1,64,8192]{2,1,0:T(8,128)(2,1)} %param.7) | copy-start | bytes 3145732
  54.2 28.6 %all-to-all-start = ((bf16[2,64,8192]{2,1,0:T(8,128)(2,1)}), bf16[2,64,8192]{2,1,0:T(8,128)(2,1)S(1)}, u32[]{:S(2)}, u32[]{:S(2)}) async-start(bf16[2,64,8192]{2,1,0:T(8,128)(2,1)} %bitcast.14), calls=%async_computation.1 | async-start | bytes 4194304 | tf_op jit(solution)/shard_map/all_to_all | solution.py:67
  58.1 60.3 %all-gather.4.cloned.1.call-start = ((), (), s32[]{:S(2)}) async-start(), calls=%async_computation.2 | async-start | bytes 3145728 | tf_op jit(solution)/shard_map/all_gather | solution.py:48
  85.7 107.3 %reduce-scatter.2.cloned.1.call-start = ((), (), s32[]{:S(2)}) async-start(), calls=%async_computation.3 | async-start | bytes 4718592 | tf_op jit(solution)/shard_map/reduce_scatter | solution.py:51
  123.2 69.7 %collective-permute-start = (bf16[64,8192]{1,0:T(8,128)(2,1)S(1)}, bf16[64,8192]{1,0:T(8,128)(2,1)S(1)}, u32[]{:S(2)}, u32[]{:S(2)}) collective-permute-start(bf16[64,8192]{1,0:T(8,128)(2,1)S(1)} %get-tuple-element.5), channel_id=1, source_target_pairs={{16,0},{17,1},{18,2},{19,3},{20,4},{21,5},{22,6},{23,7},{24,8},{25... | collective-permute-start | bytes 3145736 | tf_op jit(solution)/shard_map/ppermute | solution.py:15
Sparse Core Ops, SparseCore 0:
  9.9 39.2 all-gather.5
  85.8 32.5 all-gather.3
  123.4 51.3 reduce-scatter.1
where the time goes:
time: 205 us; the launch traced here: 203 us
  waiting for transfers between devices  94.7 us (46%)
  blocking collectives  68.4 us (33%)
  between operations  13.8 us (7%)
  matrix products  10.7 us (5%)
  other arithmetic  5.36 us (3%)
  starting transfers between devices  5.31 us (3%)
  local copies, waits for them, and re-layouts  4.3 us (2%)
    psum x1, blocking collectives, shards(): gain_grad = lax.psum(jnp.sum(own_grad * normed, axis=0), ('dp', 'tensor'))  68.4 us
    all_gather x1, waiting for transfers between devices, shards(): lax.all_gather(local_weight, 'dp', axis=0, tiled=True)  37 us
    all_gather x1, waiting for transfers between devices, shards(): layer_input = lax.all_gather(own_input, 'tensor', axis=0, tiled=True)  32.7 us
    all_to_all x1, waiting for transfers between devices, shards(): lax.all_to_all(stacked, 'tensor', split_axis=0, concat_axis=0, tiled=True)  24.3 us
    dot_general x1, matrix products, shards(): jnp.einsum('tk,ck->tc', value_grad, lax.all_gather(local_weight, 'dp', ax...  5.02 us
    dot_general x1, matrix products, shards(): jnp.einsum('tc,tk->ck', layer_input, value_grad, preferred_element_type=j...  4.8 us
  transfers between devices with their start and end apart: 5, of which 3 were waited for; matrix products, arithmetic and copies ran while one was open for 2% of the time, Pallas kernels for 0%

commit v1 on v0

v1 whole, which is shorter than its diff:
```python
import functools
import math

import jax
import jax.numpy as jnp
from jax import lax
from jax.experimental import pallas as pl
from jax.experimental.pallas import tpu as pltpu
from jax.sharding import PartitionSpec as P

HD = 128
QPK = 8
LANES = 128
MESH = pl.DeviceIdType.MESH


def dot(left, right, dims):
    return lax.dot_general(left, right, (dims, ((), ())), preferred_element_type=jnp.float32)


def kernel(
    sizes, hidden, gain, weight, query, key, grad, positions,
    weight_out, gain_out, previous,
    hid, values, value_own, weights, grad_in, inverse, stats, finished, term_send, term_recv,
    gain_parts,
    hid_send, hid_recv, wt_send, wt_recv, val_send, val_recv, stat_send, stat_recv,
    out_send, out_recv, term_ssem, term_rsem, gain_send, gain_recv, local_sem,
):
    ns, nd, nt = sizes
    section, me, col = (lax.axis_index(axis) for axis in ("section", "dp", "tensor"))
    rows = hidden.shape[1]
    features = weight.shape[1]
    width = weight.shape[2]
    tokens = rows * nd
    model = features * nd
    blocks = tokens // LANES
    per_block = LANES // rows
    chunk = min(256, features)
    chunks = features // chunk

    def dp_peer(step):
        return lax.rem(me + step, nd)

    def col_peer(step):
        return lax.rem(col + step, nt)

    barrier = pltpu.get_barrier_semaphore()

    def greet(step, carry):
        target = lax.rem(me * nt + col + step, nd * nt)
        pl.semaphore_signal(
            barrier, inc=1, device_id={"dp": target // nt, "tensor": lax.rem(target, nt)},
            device_id_type=MESH,
        )
        return carry

    lax.fori_loop(1, nd * nt, greet, 0)

    @pl.when(section < ns - 1)
    def _():
        def greet_next(step, carry):
            pl.semaphore_signal(
                barrier, inc=1, device_id={"section": section + 1, "dp": dp_peer(step)},
                device_id_type=MESH,
            )
            return carry

        lax.fori_loop(0, nd, greet_next, 0)

    pl.semaphore_wait(barrier, nd * nt - 1 + nd * jnp.minimum(section, 1))

    def row_slice(index):
        return pl.ds(pl.multiple_of(index * rows, rows), rows)

    def feature_slice(index):
        return pl.ds(pl.multiple_of(index * features, features), features)

    def hid_copy(target, source):
        return pltpu.make_async_remote_copy(
            src_ref=hidden.at[0, :, feature_slice(target)], dst_ref=hid.at[row_slice(source), :],
            send_sem=hid_send.at[target], recv_sem=hid_recv.at[source],
            device_id={"dp": target}, device_id_type=MESH,
        )

    def weight_copy(target, source):
        return pltpu.make_async_remote_copy(
            src_ref=weight.at[0], dst_ref=weights.at[source],
            send_sem=wt_send.at[target], recv_sem=wt_recv.at[source],
            device_id={"tensor": target}, device_id_type=MESH,
        )

    def value_copy(target_dp, target_col, source_dp, source_col):
        return pltpu.make_async_remote_copy(
            src_ref=value_own.at[target_col],
            dst_ref=values.at[source_col, row_slice(source_dp), :],
            send_sem=val_send.at[target_col, target_dp], recv_sem=val_recv.at[source_col, source_dp],
            device_id={"dp": target_dp, "tensor": target_col}, device_id_type=MESH,
        )

    def stat_copy(target, source):
        return pltpu.make_async_remote_copy(
            src_ref=stats.at[me], dst_ref=stats.at[source],
            send_sem=stat_send.at[target], recv_sem=stat_recv.at[source],
            device_id={"dp": target}, device_id_type=MESH,
        )

    def out_copy(target, source):
        return pltpu.make_async_remote_copy(
            src_ref=finished.at[row_slice(target), :],
            dst_ref=previous.at[:, feature_slice(source)],
            send_sem=out_send.at[target], recv_sem=out_recv.at[source],
            device_id={"section": jnp.maximum(section - 1, 0), "dp": target}, device_id_type=MESH,
        )

    def term_copy(target, source):
        return pltpu.make_async_remote_copy(
            src_ref=term_send.at[target], dst_ref=term_recv.at[source],
            send_sem=term_ssem.at[target], recv_sem=term_rsem.at[source],
            device_id={"tensor": target}, device_id_type=MESH,
        )

    def gain_copy(target_dp, target_col, source_dp, source_col):
        return pltpu.make_async_remote_copy(
            src_ref=gain_parts.at[col, me], dst_ref=gain_parts.at[source_col, source_dp],
            send_sem=gain_send.at[target_col, target_dp],
            recv_sem=gain_recv.at[source_col, source_dp],
            device_id={"dp": target_dp, "tensor": target_col}, device_id_type=MESH,
        )

    def loop(first, last, body):
        def run(step, carry):
            body(step)
            return carry

        lax.fori_loop(first, last, run, 0)

    def over_section(body):
        def run(step):
            target = lax.rem(me * nt + col + step, nd * nt)
            body(target // nt, lax.rem(target, nt))

        loop(1, nd * nt, run)

    loop(1, nd, lambda step: hid_copy(dp_peer(step), me).start())
    loop(1, nt, lambda step: weight_copy(col_peer(step), col).start())
    own_hid = pltpu.make_async_copy(
        hidden.at[0, :, feature_slice(me)], hid.at[row_slice(me), :], local_sem.at[0]
    )
    own_hid.start()
    own_weight = pltpu.make_async_copy(weight.at[0], weights.at[col], local_sem.at[1])
    own_weight.start()

    @pl.when(section == ns - 1)
    def _():
        previous[...] = jnp.zeros_like(previous)

    length = query.shape[1]
    down = lax.broadcasted_iota(jnp.int32, (length, length), 0)
    across = lax.broadcasted_iota(jnp.int32, (length, length), 1)
    base_across = jnp.broadcast_to(positions[...], (length, length)) - across
    visible = (down <= across) & (base_across == base_across.T)
    for group in range(width // HD):
        key_rows = key[0, :, group * HD : (group + 1) * HD]
        total = jnp.zeros((length, HD), jnp.float32)
        for head in range(QPK):
            first = (group * QPK + head) * HD
            scores = dot(key_rows, query[0, :, first : first + HD], ((1,), (1,)))
            masked = jnp.where(visible, scores / math.sqrt(HD), jnp.float32(-1e30))
            largest = jnp.max(masked, axis=0, keepdims=True)
            powers = jnp.where(visible, jnp.exp(masked - largest), jnp.float32(0.0))
            probabilities = powers / jnp.sum(powers, axis=0, keepdims=True)
            total = total + dot(
                probabilities.astype(jnp.bfloat16), grad[0, :, first : first + HD], ((1,), (0,))
            )
        rounded = total.astype(jnp.bfloat16)
        for part in range(nt):
            value_own[part, :, group * HD : (group + 1) * HD] = rounded[
                part * rows : (part + 1) * rows
            ]

    over_section(lambda dp, tensor: value_copy(dp, tensor, me, col).start())
    values[col, row_slice(me), :] = value_own[col]

    own_hid.wait()
    own_weight.wait()
    loop(1, nt, lambda step: weight_copy(col_peer(step), col_peer(step)).wait_recv())
    loop(1, nd, lambda step: hid_copy(dp_peer(step), dp_peer(step)).wait_recv())
    over_section(lambda dp, tensor: value_copy(dp, tensor, dp, tensor).wait_recv())

    def gain_row(start, size):
        place = pl.multiple_of(me * features + start, LANES)
        return gain[:, pl.ds(place, size)].astype(jnp.float32)

    def fold(array):
        out = array[:, :LANES]
        for at in range(LANES, array.shape[1], LANES):
            out = out + array[:, at : at + LANES]
        return out

    products = [jnp.zeros((LANES, LANES), jnp.float32) for _ in range(blocks)]
    squares = [jnp.zeros((LANES, LANES), jnp.float32) for _ in range(blocks)]
    for piece in range(chunks):
        at = piece * chunk
        terms = jnp.zeros((tokens, chunk), jnp.float32)
        for part in range(nt):
            terms = terms + dot(values[part], weights[part, at : at + chunk, :], ((1,), (1,)))
        grad_in[:, at : at + chunk] = terms
        scaled = gain_row(at, chunk)
        for block in range(blocks):
            span = slice(block * LANES, (block + 1) * LANES)
            inputs = hid[span, at : at + chunk].astype(jnp.float32)
            products[block] = products[block] + fold(terms[span] * scaled * inputs)
            squares[block] = squares[block] + fold(inputs * inputs)
    for block in range(blocks):
        stats[me, block : block + 1, :] = jnp.sum(products[block].T, axis=0, keepdims=True)
        stats[me, blocks + block : blocks + block + 1, :] = jnp.sum(
            squares[block].T, axis=0, keepdims=True
        )

    loop(1, nd, lambda step: stat_copy(dp_peer(step), me).start())
    loop(1, nd, lambda step: stat_copy(dp_peer(step), dp_peer(step)).wait_recv())

    totals = stats[0]
    for index in range(1, nd):
        totals = totals + stats[index]
    mean_square = totals[blocks:] / model + 1e-05
    root = jnp.sqrt(mean_square)
    stretch = 1.0 / root
    inner = totals[:blocks] / model / mean_square

    def column(rows_of, block):
        return jnp.broadcast_to(rows_of[block : block + 1], (LANES, LANES)).T

    for block in range(blocks):
        span = slice(block * LANES, (block + 1) * LANES)
        inverse[0, span, :] = column(stretch, block)
        inverse[1, span, :] = column(inner, block)

    def finish(step):
        block = lax.rem(me // per_block + step, blocks)
        span = pl.ds(pl.multiple_of(block * LANES, LANES), LANES)
        scale = inverse[0, span, :]
        mean = inverse[1, span, :]
        for at in range(0, features, LANES):
            lanes = slice(at, at + LANES)
            normal = grad_in[span, lanes] * gain_row(at, LANES)
            inputs = hid[span, lanes].astype(jnp.float32)
            finished[span, lanes] = ((normal - inputs * mean) * scale).astype(jnp.bfloat16)

        @pl.when(section > 0)
        def _():
            for part in range(per_block):
                out_copy(block * per_block + part, me).start()

    loop(0, blocks, finish)

    for piece in range(chunks):
        at = piece * chunk
        scaled = gain_row(at, chunk)
        parts = []
        sums = jnp.zeros((1, chunk), jnp.float32)
        for block in range(blocks):
            span = slice(block * LANES, (block + 1) * LANES)
            scale = jnp.concatenate([inverse[0, span, :]] * (chunk // LANES), axis=1)
            normed = hid[span, at : at + chunk].astype(jnp.float32) * scale
            parts.append((normed * scaled).astype(jnp.bfloat16))
            sums = sums + jnp.sum(
                grad_in[span, at : at + chunk] * normed, axis=0, keepdims=True
            )
        gain_parts[col, me, :, at : at + chunk] = sums
        inputs = jnp.concatenate(parts, axis=0)
        weight_out[0, at : at + chunk, :] = dot(inputs, values[col], ((0,), (0,)))
        for step in range(1, nt):
            target = col_peer(step)
            term_send[target, at : at + chunk, :] = dot(
                inputs, values[target], ((0,), (0,))
            ).astype(jnp.bfloat16)

    loop(1, nt, lambda step: term_copy(col_peer(step), col).start())
    over_section(lambda dp, tensor: gain_copy(dp, tensor, me, col).start())

    for step in range(1, nt):
        term_copy(col_peer(step), col_peer(step)).wait_recv()
        weight_out[0] += term_recv[col_peer(step)].astype(jnp.float32)
    over_section(lambda dp, tensor: gain_copy(dp, tensor, dp, tensor).wait_recv())
    for index in range(nd):
        total = gain_parts[0, index]
        for part in range(1, nt):
            total = total + gain_parts[part, index]
        gain_out[:, index * features : (index + 1) * features] = total

    loop(1, nd, lambda step: hid_copy(dp_peer(step), me).wait_send())
    loop(1, nt, lambda step: weight_copy(col_peer(step), col).wait_send())
    over_section(lambda dp, tensor: value_copy(dp, tensor, me, col).wait_send())
    loop(1, nd, lambda step: stat_copy(dp_peer(step), me).wait_send())
    loop(1, nt, lambda step: term_copy(col_peer(step), col).wait_send())
    over_section(lambda dp, tensor: gain_copy(dp, tensor, me, col).wait_send())

    @pl.when(section < ns - 1)
    def _():
        loop(0, nd, lambda step: out_copy(dp_peer(step), dp_peer(step)).wait_recv())

    @pl.when(section > 0)
    def _():
        loop(0, nd, lambda step: out_copy(dp_peer(step), me).wait_send())


def shards(sizes, hidden_in, norm_gain, value_weight, query, key, grad, positions):
    ns, nd, nt = sizes
    rows, model = hidden_in.shape[1:]
    features, width = value_weight.shape[1:]
    tokens = rows * nd
    vmem = pl.BlockSpec(memory_space=pltpu.VMEM)
    dma = pltpu.SemaphoreType.DMA
    return pl.pallas_call(
        functools.partial(kernel, sizes),
        out_shape=(
            jax.ShapeDtypeStruct(value_weight.shape, jnp.float32),
            jax.ShapeDtypeStruct(norm_gain.shape, jnp.float32),
            jax.ShapeDtypeStruct((rows, model), jnp.bfloat16),
        ),
        in_specs=[vmem] * 7,
        out_specs=(vmem, vmem, vmem),
        scratch_shapes=[
            pltpu.VMEM((tokens, features), jnp.bfloat16),
            pltpu.VMEM((nt, tokens, width), jnp.bfloat16),
            pltpu.VMEM((nt, rows, width), jnp.bfloat16),
            pltpu.VMEM((nt, features, width), jnp.bfloat16),
            pltpu.VMEM((tokens, features), jnp.float32),
            pltpu.VMEM((2, tokens, LANES), jnp.float32),
            pltpu.VMEM((nd, 2 * tokens // LANES, LANES), jnp.float32),
            pltpu.VMEM((tokens, features), jnp.bfloat16),
            pltpu.VMEM((nt, features, width), jnp.bfloat16),
            pltpu.VMEM((nt, features, width), jnp.bfloat16),
            pltpu.VMEM((nt, nd, 1, features), jnp.float32),
            dma((nd,)), dma((nd,)), dma((nt,)), dma((nt,)),
            dma((nt, nd)), dma((nt, nd)), dma((nd,)), dma((nd,)),
            dma((nd,)), dma((nd,)), dma((nt,)), dma((nt,)),
            dma((nt, nd)), dma((nt, nd)), dma((2,)),
        ],
        compiler_params=pltpu.CompilerParams(
            collective_id=0, has_side_effects=True, vmem_limit_bytes=48 * 1024 * 1024
        ),
        name="value_path_backward",
    )(hidden_in, norm_gain, value_weight, query, key, grad, positions)


def solution(mesh):
    sizes = tuple(mesh.shape[axis] for axis in ("section", "dp", "tensor"))

    def local(hidden_in, norm_gain, value_weight, query, key, grad, positions):
        weight_grad, gain_grad, previous = shards(
            sizes, hidden_in, norm_gain, value_weight, query, key, grad, positions
        )
        return (weight_grad, gain_grad, previous[None])

    return jax.shard_map(
        local,
        mesh=mesh,
        in_specs=(
            P("section", ("dp", "tensor"), None),
            P("section", None),
            P("section", "dp", "tensor"),
            P("section", "dp", "tensor"),
            P("section", "dp", "tensor"),
            P("section", "dp", "tensor"),
            P("section", "dp"),
        ),
        out_specs=(
            P("section", "dp", "tensor"),
            P("section", None),
            P("section", ("dp", "tensor"), None),
        ),
        check_vma=False,
    )
```

time: 205 us -> 87.5 us (0.43)
  waiting for transfers between devices: 94.7 us -> 0 us
  Pallas kernels: 0 us -> 77.2 us
  blocking collectives: 68.4 us -> 0 us
  between operations: 13.8 us -> 0.66 us
  matrix products: 10.7 us -> 0 us
  other arithmetic: 5.36 us -> 0 us
  starting transfers between devices: 5.31 us -> 0 us
  local copies, waits for them, and re-layouts: 4.3 us -> 9.15 us
    pallas_call x0 -> x1, Pallas kernels: none -> 77.2 us  [shards(): pl.pallas_call(functools.partial(kernel, sizes), out_shape=(jax.ShapeDtyp...]
    all_gather x2 -> x0, waiting for transfers between devices: 69.7 us -> none  [the longest x1 37 us: shards(): lax.all_gather(local_weight, 'dp', axis=0, tiled=True)]
    psum x1 -> x0, blocking collectives: 68.4 us -> none  [shards(): gain_grad = lax.psum(jnp.sum(own_grad * normed, axis=0), ('dp', 'tensor'))]
    all_to_all x1 -> x0, waiting for transfers between devices: 24.3 us -> none  [shards(): lax.all_to_all(stacked, 'tensor', split_axis=0, concat_axis=0, tiled=True)]
    dot_general x3 -> x0, matrix products: 10.1 us -> none  [the longest x1 5.02 us: shards(): jnp.einsum('tk,ck->tc', value_grad, lax.all_gather(local_weight, 'dp', ax...]
    unnamed x8 -> x17, local copies, waits for them, and re-layouts: 2.13 us -> 9.15 us
    all_to_all x1 -> x0, starting transfers between devices: 3.89 us -> none  [shards(): lax.all_to_all(stacked, 'tensor', split_axis=0, concat_axis=0, tiled=True)]
    another operation x2 -> x0, local copies, waits for them, and re-layouts: 2.17 us -> none  [the longest x1 1.31 us: attend(): grad_heads = grad_rows.reshape(length, groups, QPK, HD)]
  transfers between devices with their start and end apart: 5 -> 0, of which waited for: 3 -> 0; matrix products, arithmetic and copies ran while one was open for 2% -> 0% of each run, Pallas kernels for 0% -> 0%
where the time goes in v1:
time: 87.5 us; the launch traced here: 87.1 us
  Pallas kernels  77.2 us (88%)
  local copies, waits for them, and re-layouts  9.15 us (10%)
    pallas_call x1, Pallas kernels, shards(): pl.pallas_call(functools.partial(kernel, sizes), out_shape=(jax.ShapeDtyp...  77.2 us
    unnamed x17, local copies, waits for them, and re-layouts  9.15 us

profile of v1, /device:TPU:1, one launch (start us, length us, event | category | flops | bytes accessed | tf_op | source)
XLA Modules:
  0.0 87.1 jit_solution(5510968338963087309)
XLA Ops:
  0.6 0.0 copy-start
  0.6 1.2 %copy-done = bf16[1,64,8192]{2,1,0:T(8,128)(2,1)S(1)} copy-done((bf16[1,64,8192]{2,1,0:T(8,128)(2,1)S(1)}, bf16[1,64,8192]{2,1,0:T(8,128)(2,1)}, u32[]{:S(2)}) %copy-start) | copy-done | bytes 1048600
  1.9 0.0 copy-start.1
  1.9 1.0 %copy-done.1 = bf16[1,1024,256]{2,1,0:T(8,128)(2,1)S(1)} copy-done((bf16[1,1024,256]{2,1,0:T(8,128)(2,1)S(1)}, bf16[1,1024,256]{2,1,0:T(8,128)(2,1)}, u32[]{:S(2)}) %copy-start.1) | copy-done | bytes 524312
  2.9 0.0 copy-start.2
  2.9 1.0 %copy-done.2 = bf16[1,128,2048]{2,1,0:T(8,128)(2,1)S(1)} copy-done((bf16[1,128,2048]{2,1,0:T(8,128)(2,1)S(1)}, bf16[1,128,2048]{2,1,0:T(8,128)(2,1)}, u32[]{:S(2)}) %copy-start.2) | copy-done | bytes 524312
  3.9 0.0 copy-start.3
  3.9 1.0 %copy-done.3 = bf16[1,128,2048]{2,1,0:T(8,128)(2,1)S(1)} copy-done((bf16[1,128,2048]{2,1,0:T(8,128)(2,1)S(1)}, bf16[1,128,2048]{2,1,0:T(8,128)(2,1)}, u32[]{:S(2)}) %copy-start.3) | copy-done | bytes 524312
  5.0 0.0 copy-start.4
  5.0 0.8 copy-done.4
  5.8 0.0 copy-start.5
  5.8 0.8 copy-done.5
  6.6 0.0 copy-start.6
  6.6 0.7 copy-done.6
  7.2 77.2 %value_path_backward.1 = (f32[1,1024,256]{2,1,0:T(8,128)S(1)}, f32[1,8192]{1,0:T(1,128)S(1)}, bf16[64,8192]{1,0:T(8,128)(2,1)S(1)}) custom-call(bf16[1,64,8192]{2,1,0:T(8,128)(2,1)S(1)} %copy-done, bf16[1,8192]{1,0:T(2,128)(2,1)S(1)} %copy-done.5, bf16[1,1024,256]{2,1,0:T(8,128)(2,1)S(1)} %copy-done.1, bf16[1,128,2048]{2,1,0:T(8,128)(2,1)S(1)} %copy-done.2, ...), custom_call_target="tpu_custom_call" | custom-call | tf_op jit(solution)/shard_map/value_path_backward/pallas_call | solution.py:315
  84.5 1.0 %copy.13 = f32[1,1024,256]{2,1,0:T(8,128)} copy(f32[1,1024,256]{2,1,0:T(8,128)S(1)} %get-tuple-element.12) | data formatting | bytes 2097152
  85.5 0.6 copy.14
  86.1 1.0 %copy.15 = bf16[1,64,8192]{2,1,0:T(8,128)(2,1)} copy(bf16[1,64,8192]{2,1,0:T(8,128)(2,1)S(1)} %bitcast.1) | data formatting | bytes 2097152
Async XLA Ops:
  0.6 1.2 %copy-start = (bf16[1,64,8192]{2,1,0:T(8,128)(2,1)S(1)}, bf16[1,64,8192]{2,1,0:T(8,128)(2,1)}, u32[]{:S(2)}) copy-start(bf16[1,64,8192]{2,1,0:T(8,128)(2,1)} %hidden.1) | copy-start | bytes 3145732
  1.9 1.0 %copy-start.1 = (bf16[1,1024,256]{2,1,0:T(8,128)(2,1)S(1)}, bf16[1,1024,256]{2,1,0:T(8,128)(2,1)}, u32[]{:S(2)}) copy-start(bf16[1,1024,256]{2,1,0:T(8,128)(2,1)} %weight.1) | copy-start | bytes 1572868
  2.9 1.0 %copy-start.2 = (bf16[1,128,2048]{2,1,0:T(8,128)(2,1)S(1)}, bf16[1,128,2048]{2,1,0:T(8,128)(2,1)}, u32[]{:S(2)}) copy-start(bf16[1,128,2048]{2,1,0:T(8,128)(2,1)} %query.1) | copy-start | bytes 1572868
  3.9 1.0 %copy-start.3 = (bf16[1,128,2048]{2,1,0:T(8,128)(2,1)S(1)}, bf16[1,128,2048]{2,1,0:T(8,128)(2,1)}, u32[]{:S(2)}) copy-start(bf16[1,128,2048]{2,1,0:T(8,128)(2,1)} %grad.1) | copy-start | bytes 1572868
  5.0 0.8 copy-start.4
  5.8 0.8 copy-start.5
  6.6 0.7 copy-start.6

commit v2 on v1

v2 whole, which is shorter than its diff:
```python
import functools
import math

import jax
import jax.numpy as jnp
from jax import lax
from jax.experimental import pallas as pl
from jax.experimental.pallas import tpu as pltpu
from jax.sharding import PartitionSpec as P

HD = 128
QPK = 8
PARTS = 2
LANES = 128
MESH = pl.DeviceIdType.MESH


def dot(left, right, dims):
    return lax.dot_general(left, right, (dims, ((), ())), preferred_element_type=jnp.float32)


def kernel(
    sizes, hidden, gain, weight, query_hbm, key_hbm, grad_hbm, positions_hbm,
    weight_out, gain_out, previous,
    query, key, grad, positions, hid, values, value_own, weights, grad_in, inverse, stats, finished, term_send, term_recv,
    gain_parts,
    hid_send, hid_recv, wt_send, wt_recv, val_send, val_recv, stat_send, stat_recv,
    out_send, out_recv, term_ssem, term_rsem, gain_send, gain_recv, local_sem,
):
    ns, nd, nt = sizes
    section, me, col = (lax.axis_index(axis) for axis in ("section", "dp", "tensor"))
    rows = hidden.shape[1]
    features = weight.shape[1]
    width = weight.shape[2]
    sub = rows // PARTS
    tokens = sub * nd
    model = features * nd
    blocks = tokens // LANES
    chunk = min(256, features)
    chunks = features // chunk

    def dp_peer(step):
        return lax.rem(me + step, nd)

    def col_peer(step):
        return lax.rem(col + step, nt)

    fetches = [
        pltpu.make_async_copy(source, target, local_sem.at[1 + index])
        for index, (source, target) in enumerate(
            [
                (positions_hbm, positions), (key_hbm.at[0], key),
                (query_hbm.at[0], query), (grad_hbm.at[0], grad),
            ]
        )
    ]
    for fetch in fetches:
        fetch.start()

    barrier = pltpu.get_barrier_semaphore()

    def greet(step, carry):
        target = lax.rem(me * nt + col + step, nd * nt)
        pl.semaphore_signal(
            barrier, inc=1, device_id={"dp": target // nt, "tensor": lax.rem(target, nt)},
            device_id_type=MESH,
        )
        return carry

    lax.fori_loop(1, nd * nt, greet, 0)

    @pl.when(section < ns - 1)
    def _():
        def greet_next(step, carry):
            pl.semaphore_signal(
                barrier, inc=1, device_id={"section": section + 1, "dp": dp_peer(step)},
                device_id_type=MESH,
            )
            return carry

        lax.fori_loop(0, nd, greet_next, 0)

    pl.semaphore_wait(barrier, nd * nt - 1 + nd * jnp.minimum(section, 1))

    def row_slice(index):
        return pl.ds(pl.multiple_of(index * sub, sub), sub)

    def feature_slice(index):
        return pl.ds(pl.multiple_of(index * features, features), features)

    def hid_copy(part, target, source):
        return pltpu.make_async_remote_copy(
            src_ref=hidden.at[0, part * sub : (part + 1) * sub, feature_slice(target)],
            dst_ref=hid.at[part, row_slice(source), :],
            send_sem=hid_send.at[part, target], recv_sem=hid_recv.at[part, source],
            device_id={"dp": target}, device_id_type=MESH,
        )

    def weight_copy(target, source):
        return pltpu.make_async_remote_copy(
            src_ref=weight.at[0], dst_ref=weights.at[source],
            send_sem=wt_send.at[target], recv_sem=wt_recv.at[source],
            device_id={"tensor": target}, device_id_type=MESH,
        )

    def value_copy(part, target_dp, target_col, source_dp, source_col):
        return pltpu.make_async_remote_copy(
            src_ref=value_own.at[target_col, part],
            dst_ref=values.at[part, source_col, row_slice(source_dp), :],
            send_sem=val_send.at[part, target_col, target_dp],
            recv_sem=val_recv.at[part, source_col, source_dp],
            device_id={"dp": target_dp, "tensor": target_col}, device_id_type=MESH,
        )

    def stat_copy(part, target, source):
        return pltpu.make_async_remote_copy(
            src_ref=stats.at[part, me], dst_ref=stats.at[part, source],
            send_sem=stat_send.at[part, target], recv_sem=stat_recv.at[part, source],
            device_id={"dp": target}, device_id_type=MESH,
        )

    def out_copy(part, target, source):
        return pltpu.make_async_remote_copy(
            src_ref=finished.at[part, row_slice(target), :],
            dst_ref=previous.at[part * sub : (part + 1) * sub, feature_slice(source)],
            send_sem=out_send.at[part, target], recv_sem=out_recv.at[part, source],
            device_id={"section": jnp.maximum(section - 1, 0), "dp": target}, device_id_type=MESH,
        )

    def term_copy(target, source):
        return pltpu.make_async_remote_copy(
            src_ref=term_send.at[target], dst_ref=term_recv.at[source],
            send_sem=term_ssem.at[target], recv_sem=term_rsem.at[source],
            device_id={"tensor": target}, device_id_type=MESH,
        )

    def gain_copy(target_dp, target_col, source_dp, source_col):
        return pltpu.make_async_remote_copy(
            src_ref=gain_parts.at[col, me], dst_ref=gain_parts.at[source_col, source_dp],
            send_sem=gain_send.at[target_col, target_dp],
            recv_sem=gain_recv.at[source_col, source_dp],
            device_id={"dp": target_dp, "tensor": target_col}, device_id_type=MESH,
        )

    def loop(first, last, body):
        def run(step, carry):
            body(step)
            return carry

        lax.fori_loop(first, last, run, 0)

    def over_section(body):
        def run(step):
            target = lax.rem(me * nt + col + step, nd * nt)
            body(target // nt, lax.rem(target, nt))

        loop(1, nd * nt, run)

    loop(1, nd, lambda step: hid_copy(0, dp_peer(step), me).start())
    loop(1, nt, lambda step: weight_copy(col_peer(step), col).start())
    own_hid = [
        pltpu.make_async_copy(
            hidden.at[0, part * sub : (part + 1) * sub, feature_slice(me)],
            hid.at[part, row_slice(me), :], hid_recv.at[part, me],
        )
        for part in range(PARTS)
    ]
    for copy in own_hid:
        copy.start()
    own_weight = pltpu.make_async_copy(weight.at[0], weights.at[col], local_sem.at[0])
    own_weight.start()

    @pl.when(section == ns - 1)
    def _():
        previous[...] = jnp.zeros_like(previous)

    for fetch in fetches:
        fetch.wait()
    length = query.shape[0]
    down = lax.broadcasted_iota(jnp.int32, (length, length), 0)
    across = lax.broadcasted_iota(jnp.int32, (length, length), 1)
    base_across = jnp.broadcast_to(positions[...], (length, length)) - across
    visible = (down <= across) & (base_across == base_across.T)
    for group in range(width // HD):
        key_rows = key[:, group * HD : (group + 1) * HD]
        total = jnp.zeros((length, HD), jnp.float32)
        for head in range(QPK):
            first = (group * QPK + head) * HD
            scores = dot(key_rows, query[:, first : first + HD], ((1,), (1,)))
            masked = jnp.where(visible, scores / math.sqrt(HD), jnp.float32(-1e30))
            largest = jnp.max(masked, axis=0, keepdims=True)
            powers = jnp.where(visible, jnp.exp(masked - largest), jnp.float32(0.0))
            probabilities = powers / jnp.sum(powers, axis=0, keepdims=True)
            total = total + dot(
                probabilities.astype(jnp.bfloat16), grad[:, first : first + HD], ((1,), (0,))
            )
        rounded = total.astype(jnp.bfloat16)
        for tensor in range(nt):
            for part in range(PARTS):
                first = tensor * rows + part * sub
                value_own[tensor, part, :, group * HD : (group + 1) * HD] = rounded[
                    first : first + sub
                ]

    def send_values(part):
        over_section(lambda dp, tensor: value_copy(part, dp, tensor, me, col).start())
        values[part, col, row_slice(me), :] = value_own[col, part]

    def send_later():
        for part in range(1, PARTS):
            loop(1, nd, lambda step: hid_copy(part, dp_peer(step), me).start())
            send_values(part)

    send_values(0)
    send_later()
    own_weight.wait()
    loop(1, nt, lambda step: weight_copy(col_peer(step), col_peer(step)).wait_recv())

    def gain_row(start, size):
        place = pl.multiple_of(me * features + start, LANES)
        return gain[:, pl.ds(place, size)].astype(jnp.float32)

    def fold(array):
        out = array[:, :LANES]
        for at in range(LANES, array.shape[1], LANES):
            out = out + array[:, at : at + LANES]
        return out

    def column(rows_of, block):
        return jnp.broadcast_to(rows_of[block : block + 1], (LANES, LANES)).T

    def multiply(part):
        own_hid[part].wait()
        loop(1, nd, lambda step: hid_copy(part, dp_peer(step), dp_peer(step)).wait_recv())
        over_section(lambda dp, tensor: value_copy(part, dp, tensor, dp, tensor).wait_recv())
        products = [jnp.zeros((LANES, LANES), jnp.float32) for _ in range(blocks)]
        squares = [jnp.zeros((LANES, LANES), jnp.float32) for _ in range(blocks)]
        for piece in range(chunks):
            at = piece * chunk
            terms = jnp.zeros((tokens, chunk), jnp.float32)
            for tensor in range(nt):
                terms = terms + dot(
                    values[part, tensor], weights[tensor, at : at + chunk, :], ((1,), (1,))
                )
            grad_in[part, :, at : at + chunk] = terms
            scaled = gain_row(at, chunk)
            for block in range(blocks):
                span = slice(block * LANES, (block + 1) * LANES)
                inputs = hid[part, span, at : at + chunk].astype(jnp.float32)
                products[block] = products[block] + fold(terms[span] * scaled * inputs)
                squares[block] = squares[block] + fold(inputs * inputs)
        for block in range(blocks):
            stats[part, me, block : block + 1, :] = jnp.sum(
                products[block].T, axis=0, keepdims=True
            )
            stats[part, me, blocks + block : blocks + block + 1, :] = jnp.sum(
                squares[block].T, axis=0, keepdims=True
            )

        loop(1, nd, lambda step: stat_copy(part, dp_peer(step), me).start())

    def finish(part):
        loop(1, nd, lambda step: stat_copy(part, dp_peer(step), dp_peer(step)).wait_recv())

        totals = stats[part, 0]
        for index in range(1, nd):
            totals = totals + stats[part, index]
        mean_square = totals[blocks:] / model + 1e-05
        stretch = 1.0 / jnp.sqrt(mean_square)
        inner = totals[:blocks] / model / mean_square

        for block in range(blocks):
            span = slice(block * LANES, (block + 1) * LANES)
            scale = column(stretch, block)
            mean = column(inner, block)
            inverse[part, span, :] = scale
            for at in range(0, features, LANES):
                lanes = slice(at, at + LANES)
                normal = grad_in[part, span, lanes] * gain_row(at, LANES)
                inputs = hid[part, span, lanes].astype(jnp.float32)
                finished[part, span, lanes] = ((normal - inputs * mean) * scale).astype(
                    jnp.bfloat16
                )

    def send_out(part, first, last):
        @pl.when(section > 0)
        def _():
            loop(first, last, lambda step: out_copy(part, dp_peer(step), me).start())

    multiply(0)
    finish(0)
    ahead = max(1, nd * 3 // 8)
    send_out(0, 0, ahead)
    multiply(1)
    send_out(0, ahead, nd)
    finish(1)
    send_out(1, 0, nd)

    for piece in range(chunks):
        at = piece * chunk
        scaled = gain_row(at, chunk)
        inputs = []
        sums = jnp.zeros((1, chunk), jnp.float32)
        for part in range(PARTS):
            pieces = []
            for block in range(blocks):
                span = slice(block * LANES, (block + 1) * LANES)
                scale = jnp.concatenate([inverse[part, span, :]] * (chunk // LANES), axis=1)
                normed = hid[part, span, at : at + chunk].astype(jnp.float32) * scale
                pieces.append((normed * scaled).astype(jnp.bfloat16))
                sums = sums + jnp.sum(
                    grad_in[part, span, at : at + chunk] * normed, axis=0, keepdims=True
                )
            inputs.append(jnp.concatenate(pieces, axis=0))
        gain_parts[col, me, :, at : at + chunk] = sums
        for step in range(nt):
            target = col_peer(step)
            terms = dot(inputs[0], values[0, target], ((0,), (0,)))
            for part in range(1, PARTS):
                terms = terms + dot(inputs[part], values[part, target], ((0,), (0,)))
            if step == 0:
                weight_out[0, at : at + chunk, :] = terms
            else:
                term_send[target, at : at + chunk, :] = terms.astype(jnp.bfloat16)

    loop(1, nt, lambda step: term_copy(col_peer(step), col).start())
    over_section(lambda dp, tensor: gain_copy(dp, tensor, me, col).start())

    for step in range(1, nt):
        term_copy(col_peer(step), col_peer(step)).wait_recv()
        weight_out[0] += term_recv[col_peer(step)].astype(jnp.float32)
    over_section(lambda dp, tensor: gain_copy(dp, tensor, dp, tensor).wait_recv())
    for index in range(nd):
        total = gain_parts[0, index]
        for part in range(1, nt):
            total = total + gain_parts[part, index]
        gain_out[:, index * features : (index + 1) * features] = total

    for part in range(PARTS):
        loop(1, nd, lambda step: hid_copy(part, dp_peer(step), me).wait_send())
        over_section(lambda dp, tensor: value_copy(part, dp, tensor, me, col).wait_send())
        loop(1, nd, lambda step: stat_copy(part, dp_peer(step), me).wait_send())
    loop(1, nt, lambda step: weight_copy(col_peer(step), col).wait_send())
    loop(1, nt, lambda step: term_copy(col_peer(step), col).wait_send())
    over_section(lambda dp, tensor: gain_copy(dp, tensor, me, col).wait_send())

    @pl.when(section < ns - 1)
    def _():
        for part in range(PARTS):
            loop(0, nd, lambda step: out_copy(part, dp_peer(step), dp_peer(step)).wait_recv())

    @pl.when(section > 0)
    def _():
        for part in range(PARTS):
            loop(0, nd, lambda step: out_copy(part, dp_peer(step), me).wait_send())


def shards(sizes, hidden_in, norm_gain, value_weight, query, key, grad, positions):
    ns, nd, nt = sizes
    rows, model = hidden_in.shape[1:]
    features, width = value_weight.shape[1:]
    sub = rows // PARTS
    tokens = sub * nd
    vmem = pl.BlockSpec(memory_space=pltpu.VMEM)
    hbm = pl.BlockSpec(memory_space=pltpu.HBM)
    dma = pltpu.SemaphoreType.DMA
    return pl.pallas_call(
        functools.partial(kernel, sizes),
        out_shape=(
            jax.ShapeDtypeStruct(value_weight.shape, jnp.float32),
            jax.ShapeDtypeStruct(norm_gain.shape, jnp.float32),
            jax.ShapeDtypeStruct((rows, model), jnp.bfloat16),
        ),
        in_specs=[hbm, vmem, hbm, hbm, hbm, hbm, hbm],
        out_specs=(vmem, vmem, vmem),
        scratch_shapes=[
            pltpu.VMEM(query.shape[1:], jnp.bfloat16),
            pltpu.VMEM(key.shape[1:], jnp.bfloat16),
            pltpu.VMEM(grad.shape[1:], jnp.bfloat16),
            pltpu.VMEM(positions.shape, jnp.int32),
            pltpu.VMEM((PARTS, tokens, features), jnp.bfloat16),
            pltpu.VMEM((PARTS, nt, tokens, width), jnp.bfloat16),
            pltpu.VMEM((nt, PARTS, sub, width), jnp.bfloat16),
            pltpu.VMEM((nt, features, width), jnp.bfloat16),
            pltpu.VMEM((PARTS, tokens, features), jnp.float32),
            pltpu.VMEM((PARTS, tokens, LANES), jnp.float32),
            pltpu.VMEM((PARTS, nd, 2 * tokens // LANES, LANES), jnp.float32),
            pltpu.VMEM((PARTS, tokens, features), jnp.bfloat16),
            pltpu.VMEM((nt, features, width), jnp.bfloat16),
            pltpu.VMEM((nt, features, width), jnp.bfloat16),
            pltpu.VMEM((nt, nd, 1, features), jnp.float32),
            dma((PARTS, nd)), dma((PARTS, nd)), dma((nt,)), dma((nt,)),
            dma((PARTS, nt, nd)), dma((PARTS, nt, nd)), dma((PARTS, nd)), dma((PARTS, nd)),
            dma((PARTS, nd)), dma((PARTS, nd)), dma((nt,)), dma((nt,)),
            dma((nt, nd)), dma((nt, nd)), dma((5,)),
        ],
        compiler_params=pltpu.CompilerParams(
            collective_id=0, has_side_effects=True, vmem_limit_bytes=63 * 1024 * 1024
        ),
        name="value_path_backward",
    )(hidden_in, norm_gain, value_weight, query, key, grad, positions)


def solution(mesh):
    sizes = tuple(mesh.shape[axis] for axis in ("section", "dp", "tensor"))

    def local(hidden_in, norm_gain, value_weight, query, key, grad, positions):
        weight_grad, gain_grad, previous = shards(
            sizes, hidden_in, norm_gain, value_weight, query, key, grad, positions.reshape(1, -1)
        )
        return (weight_grad, gain_grad, previous[None])

    return jax.shard_map(
        local,
        mesh=mesh,
        in_specs=(
            P("section", ("dp", "tensor"), None),
            P("section", None),
            P("section", "dp", "tensor"),
            P("section", "dp", "tensor"),
            P("section", "dp", "tensor"),
            P("section", "dp", "tensor"),
            P("section", "dp"),
        ),
        out_specs=(
            P("section", "dp", "tensor"),
            P("section", None),
            P("section", ("dp", "tensor"), None),
        ),
        check_vma=False,
    )
```

time: 87.5 us -> 82.2 us (0.939)
  local copies, waits for them, and re-layouts: 9.15 us -> 3.94 us
    unnamed x17 -> x7, local copies, waits for them, and re-layouts: 9.15 us -> 3.94 us
where the time goes in v2:
time: 82.2 us; the launch traced here: 81.9 us
  Pallas kernels  77.3 us (94%)
  local copies, waits for them, and re-layouts  3.94 us (5%)
    pallas_call x1, Pallas kernels, shards(): pl.pallas_call(functools.partial(kernel, sizes), out_shape=(jax.ShapeDtyp...  77.3 us
    unnamed x7, local copies, waits for them, and re-layouts  3.94 us

profile of v2, /device:TPU:1, one launch (start us, length us, event | category | flops | bytes accessed | tf_op | source)
XLA Modules:
  0.0 81.9 jit_solution(14283056479765164395)
XLA Ops:
  0.6 77.3 %value_path_backward.1 = (f32[1,1024,256]{2,1,0:T(8,128)}, f32[1,8192]{1,0:T(1,128)}, bf16[64,8192]{1,0:T(8,128)(2,1)}) custom-call(bf16[1,64,8192]{2,1,0:T(8,128)(2,1)} %hidden.1, bf16[1,8192]{1,0:T(2,128)(2,1)} %gain.1, bf16[1,1024,256]{2,1,0:T(8,128)(2,1)} %weight.1, bf16[1,128,2048]{2,1,0:T(8,128)(2,1)} %query_hbm.1, bf16[1,128,256]{2,1,0:T(8,128)(2,1)} %key_hbm.1, ...), custom_call_target="tpu_custom_call" | custom-call | tf_op jit(solution)/shard_map/value_path_backward/pallas_call | solution.py:367
  77.9 0.0 copy-start.1
  78.0 0.0 copy-start
  78.0 2.4 %copy.13 = f32[1,1024,256]{2,1,0:T(8,128)} copy(f32[1,1024,256]{2,1,0:T(8,128)} %get-tuple-element.12) | data formatting | bytes 2097152
  80.3 0.0 copy-done.1
  80.3 0.6 copy.14
  80.9 0.0 copy-done
  80.9 1.0 %copy.15 = bf16[1,64,8192]{2,1,0:T(8,128)(2,1)} copy(bf16[1,64,8192]{2,1,0:T(8,128)(2,1)S(1)} %bitcast.1) | data formatting | bytes 2097152
Async XLA Ops:
  77.9 2.4 %copy-start.1 = (f32[1,8192]{1,0:T(1,128)S(1)}, f32[1,8192]{1,0:T(1,128)}, u32[]{:S(2)}) copy-start(f32[1,8192]{1,0:T(1,128)} %get-tuple-element.13) | copy-start | bytes 98308
  78.0 3.0 %copy-start = (bf16[64,8192]{1,0:T(8,128)(2,1)S(1)}, bf16[64,8192]{1,0:T(8,128)(2,1)}, u32[]{:S(2)}) copy-start(bf16[64,8192]{1,0:T(8,128)(2,1)} %get-tuple-element.8) | copy-start | bytes 3145732
